TPU v7x, 128 devices: a whole 4x4x4 slice. The times are simulated.
128 devices in a mesh: aux: 16 (over y, x), row: 4 (over z), col: 2 (over core).
Axes of the slice: x: 4, y: 4, z: 4, core: 2. Of those that a mesh axis runs over, the one named last changes fastest.
Arguments:
- integrals: bfloat16 [2560, 64, 4096], P('aux', ('row', 'col')), may hold values from -6 to 6
- pair_blocks: int32 [2, 64], P(None, ('row', 'col')), may hold values from -1 to 15, as said below
- occupied: bfloat16 [1024, 64], P('col'), may hold values from -0.75 to 0.75
- metric: bfloat16 [2560, 2560], replicated, as said below
Outputs:
- exchange_k: float32 [1024, 1024], P('row', ('aux', 'col'))
Inputs may be any that keep to these rules, and one draw needn't show every extreme that they name: `pair_blocks`: A slot of row group r and column group c (slots (r * number of column groups + c) * 8 onward) is empty (-1 in both entries) or names a row block of r's 4 blocks and a column block of c's 8 blocks; no block pair is named twice; live slots of a group come before its empty ones; every group has 4 or more live slots and some group has all 8 live. `metric`: symmetric.
All inputs are finite; a program needn't handle non-finite values.
Results may differ from a plain program's by a relative error of at most 0.0003.
Values sent between devices are 32-bit elements; how exact they have to be, the bound alone decides.
No kernel may reach another device: no remote copies, remote signals or barrier semaphores. Data moves between devices by JAX's collectives and lax.ppermute only.
A program may use at most 128 MiB of HBM per device.

v0:
```python
import jax
import jax.numpy as jnp
from jax import lax
from jax.sharding import PartitionSpec as P

NBF = 1024
BS = 64


def body(integrals, pair_blocks, occupied, metric):
    aux_rows = integrals.shape[0]
    slot_count = integrals.shape[1]
    occ_count = occupied.shape[1]
    rows_local = NBF // lax.axis_size("row")
    row_blocks = rows_local // BS
    metric_wide = metric.astype(jnp.float32)

    def add_slot(carry, slot):
        row_block = pair_blocks[0, slot]
        col_block = pair_blocks[1, slot]
        filled = row_block >= 0
        local_row = jnp.maximum(row_block, 0) % row_blocks
        local_col = jnp.maximum(col_block, 0) % (occupied.shape[0] // BS)
        tile = lax.dynamic_index_in_dim(integrals, slot, 1, False).reshape(aux_rows, BS, BS)
        cpart = lax.dynamic_slice_in_dim(occupied, local_col * BS, BS, 0)
        piece = jnp.einsum("pmn,ni->ipm", tile, cpart, preferred_element_type=jnp.float32)
        piece = jnp.where(filled, piece, 0.0)
        current = lax.dynamic_slice_in_dim(carry, local_row * BS, BS, 2)
        carry = lax.dynamic_update_slice_in_dim(carry, current + piece, local_row * BS, 2)
        return (carry, None)

    start = jnp.zeros((occ_count, aux_rows, rows_local), jnp.float32)
    partials, _ = lax.scan(add_slot, start, jnp.arange(slot_count, dtype=jnp.int32))
    summed = lax.psum_scatter(partials, "col", scatter_dimension=0, tiled=True)
    fitted = jnp.einsum(
        "qp,ipm->iqm",
        metric_wide,
        lax.all_to_all(summed, "aux", split_axis=0, concat_axis=1, tiled=True),
        precision=lax.Precision.HIGHEST,
        preferred_element_type=jnp.float32,
    )
    contrib = jnp.einsum(
        "iqm,iqn->mn",
        fitted,
        lax.all_gather(fitted, "row", axis=2, tiled=True),
        precision=lax.Precision.HIGHEST,
        preferred_element_type=jnp.float32,
    )
    return lax.psum_scatter(contrib, ("aux", "col"), scatter_dimension=1, tiled=True)


def solution(mesh):
    return jax.shard_map(
        body,
        mesh=mesh,
        in_specs=(P("aux", ("row", "col"), None), P(None, ("row", "col")), P("col", None), P()),
        out_specs=P("row", ("aux", "col")),
        check_vma=False,
    )
```

profile of v0, /device:TPU:1, one launch (start us, length us, event | category | flops | bytes accessed | tf_op | source)
XLA Modules:
  0.0 576.5 jit_solution(7274091021297569099)
XLA Ops:
  6.5 23.5 %copy.8 = bf16[160,8,4096]{0,2,1:T(8,128)(2,1)} copy(bf16[160,8,4096]{2,1,0:T(8,128)(2,1)} %param.6) | data formatting | bytes 20971520 | tf_op jit(solution)/shard_map/while | solution.py:33
  30.0 7.9 %broadcast_in_dim.11 = f32[64,160,256]{1,0,2:T(8,128)} broadcast(f32[]{:T(128)} %constant.90.clone.1), dimensions={} | broadcast | bytes 10485764 | tf_op jit(solution)/shard_map/broadcast_in_dim | solution.py:32
  37.9 91.9 %while.13 = (s32[]{:T(128)}, f32[64,160,256]{1,0,2:T(8,128)}, s32[8]{0:T(128)S(1)}, s32[2,8]{1,0:T(2,128)S(1)}, bf16[512,64]{0,1:T(8,128)(2,1)}, /*index=5*/bf16...) while((s32[]{:T(128)}, f32[64,160,256]{1,0,2:T(8,128)}, ...), condition=%wide.region_1.2_spmd, body=%wide.region_0.1_spmd.sunk | while | flops 85196824 | bytes 12338140 | solution.py:33
  42.6 1.7 constant_dynamic-slice_fusion.6
  44.4 5.0 add_dynamic-update-slice_fusion.2
  54.1 1.7 constant_dynamic-slice_fusion.6
  55.9 5.0 add_dynamic-update-slice_fusion.2
  65.6 1.7 constant_dynamic-slice_fusion.6
  67.4 5.0 add_dynamic-update-slice_fusion.2
  77.1 1.7 constant_dynamic-slice_fusion.6
  78.9 5.0 add_dynamic-update-slice_fusion.2
  88.6 1.7 constant_dynamic-slice_fusion.6
  90.4 5.0 add_dynamic-update-slice_fusion.2
  100.1 1.7 constant_dynamic-slice_fusion.6
  101.9 5.0 add_dynamic-update-slice_fusion.2
  113.3 5.0 add_dynamic-update-slice_fusion.2
  124.8 5.0 add_dynamic-update-slice_fusion.2
  129.8 15.8 %copy.9 = f32[64,160,256]{2,1,0:T(8,128)} copy(f32[64,160,256]{1,0,2:T(8,128)} %get-tuple-element.106) | data formatting | bytes 20971520 | tf_op jit(solution)/shard_map/while | solution.py:33
  145.7 25.6 %reduce-scatter.3.cloned.1.call-done = f32[32,160,256]{2,1,0:T(8,128)} async-done(((f32[64,160,256]{2,1,0:T(8,128)}), f32[32,160,256]{2,1,0:T(8,128)}) %reduce-scatter.3.cloned.1.call-update) | async-done | bytes 5242896 | tf_op jit(solution)/shard_map/reduce_scatter | solution.py:34
  171.3 68.0 %all_to_all.18 = f32[32,160,256]{2,1,0:T(8,128)S(1)} all-to-all(f32[32,160,256]{2,1,0:T(8,128)} %reduce-scatter.3.cloned.1.call-done), channel_id=1, replica_groups=mesh['aux'=16,'row'=4,'col'=2] {'aux'}, dimensions={0} | all-to-all | bytes 10485760 | tf_op jit(solution)/shard_map/all_to_all | solution.py:38
  239.7 45.5 %fusion.5 = f32[2,2560,256]{1,2,0:T(8,128)} fusion(f32[2,2560,256]{2,1,0:T(8,128)S(1)} %bitcast.41, bf16[2560,2560]{1,0:T(8,128)(2,1)} %param.9), kind=kOutput, calls=%fused_computation.9 | convolution fusion | flops 40265318400 | bytes 23592960 | tf_op jit(solution)/shard_map/qp,ipm->iqm/dot_general | solution.py:35
  285.3 186.9 %all-gather.2.cloned.1.call-done = f32[2,2560,1024]{1,2,0:T(8,128)} async-done(((f32[2,2560,256]{1,2,0:T(8,128)}), f32[2,2560,1024]{1,2,0:T(8,128)}) %all-gather.2.cloned.1.call-update) | async-done | bytes 20971536 | tf_op jit(solution)/shard_map/all_gather | solution.py:45
  472.2 21.0 %convolution_bitcast_fusion = f32[256,1024]{0,1:T(8,128)} fusion(f32[2,2560,256]{1,2,0:T(8,128)} %fusion.5, f32[2,2560,1024]{1,2,0:T(8,128)} %all-gather.2.cloned.1.call-done), kind=kOutput, calls=%fused_computation.10 | convolution fusion | flops 16106127360 | bytes 27262976 | tf_op jit(solution)/shard_map/iqm,iqn->mn/dot_general | solution.py:42
  493.2 76.8 %reduce-scatter.5.cloned.1.call-done = f32[256,32]{0,1:T(8,128)} async-done(((f32[256,1024]{0,1:T(8,128)}), f32[256,32]{0,1:T(8,128)}) %reduce-scatter.5.cloned.1.call-update) | async-done | bytes 32784 | tf_op jit(solution)/shard_map/reduce_scatter | solution.py:49
  (28 shorter events, 13.4 us)
Async XLA Ops:
  6.5 164.8 %reduce-scatter.3.cloned.1.call-start = ((), (), s32[]{:S(2)}) async-start(), calls=%async_computation.3 | async-start | bytes 15728640 | tf_op jit(solution)/shard_map/reduce_scatter | solution.py:34
  30.0 7.9 %copy-start = (s32[2,8]{1,0:T(2,128)S(1)}, s32[2,8]{1,0:T(2,128)}, u32[]{:S(2)}) copy-start(s32[2,8]{1,0:T(2,128)} %param.7) | copy-start | bytes 196
  145.7 326.5 %all-gather.2.cloned.1.call-start = ((), (), s32[]{:S(2)}) async-start(), calls=%async_computation.4 | async-start | bytes 26214400 | tf_op jit(solution)/shard_map/all_gather | solution.py:45
  285.2 284.8 %reduce-scatter.5.cloned.1.call-start = ((), (), s32[]{:S(2)}) async-start(), calls=%async_computation.5 | async-start | bytes 1081344 | tf_op jit(solution)/shard_map/reduce_scatter | solution.py:49
Sparse Core Ops, SparseCore 0:
  145.8 25.4 reduce-scatter.2
  285.3 186.8 all-gather.1
  493.3 76.6 reduce-scatter.4
where the time goes:
time: 579 us; the launch traced here: 577 us
  waiting for transfers between devices  289 us (50%)
  matrix products  106 us (18%)
  local copies, waits for them, and re-layouts  70.8 us (12%)
  blocking collectives  68 us (12%)
  loops' own time  28.7 us (5%)
  between operations  13.1 us (2%)
    all_gather x1, waiting for transfers between devices, body(): lax.all_gather(fitted, 'row', axis=2, tiled=True)  187 us
    reduce_scatter x1, waiting for transfers between devices, body(): lax.psum_scatter(contrib, ('aux', 'col'), scatter_dimension=1, tiled=True)  76.8 us
    all_to_all x1, blocking collectives, body(): lax.all_to_all(summed, 'aux', split_axis=0, concat_axis=1, tiled=True)  68 us
    dot_general x1, matrix products, body(): jnp.einsum('qp,ipm->iqm', metric_wide, lax.all_to_all(summed, 'aux', spli...  45.5 us
    dot_general x8, matrix products, add_slot(): jnp.einsum('pmn,ni->ipm', tile, cpart, preferred_element_type=jnp.float32)  39.9 us
    while x2, local copies, waits for them, and re-layouts, body(): lax.scan(add_slot, start, jnp.arange(slot_count, dtype=jnp.int32))  39.3 us
    another operation x1, loops' own time, body(): lax.scan(add_slot, start, jnp.arange(slot_count, dtype=jnp.int32))  28.7 us
    reduce_scatter x1, waiting for transfers between devices, body(): summed = lax.psum_scatter(partials, 'col', scatter_dimension=0, tiled=True)  25.6 us
  transfers between devices with their start and end apart: 3, of which 3 were waited for; matrix products, arithmetic and copies ran while one was open for 0% of the time, Pallas kernels for 0%

commit v1 on v0

v1 whole, which is shorter than its diff:
```python
import functools

import jax
import jax.numpy as jnp
from jax import lax
from jax.experimental import pallas as pl
from jax.experimental.pallas import tpu as pltpu
from jax.sharding import PartitionSpec as P

BS = 64
SLOT = 8
NOCC = 64
NAUX = 2560
AUX = 160
GROUPS = 16
CHUNKS = ((0, 80), (80, 80))
PB = 16
TILE = 512
F32 = jnp.float32
BF16 = jnp.bfloat16


def half_kernel(pairs, x_ref, occ_ref, mine_ref, other_ref, weights, wide, rhs, prod):
    @pl.when(pl.program_id(0) == 0)
    def _():
        core = lax.axis_index("col")
        row = lax.broadcasted_iota(jnp.int32, (8 * BS, 2 * BS), 0)
        lane = lax.broadcasted_iota(jnp.int32, (8 * BS, 2 * BS), 1)
        own = lax.broadcasted_iota(jnp.int32, (BS, 2 * BS), 1)
        for s in range(SLOT):
            b, e = pairs[0, s], pairs[1, s]
            local_b = jnp.where(b >= 0, lax.rem(b + 64, 4), 0)
            local_e = lax.rem(e + 64, 8)
            place = lax.rem(local_b // 2 + core, 2) * 2 + lax.rem(local_b, 2)
            place = jnp.where(b >= 0, place, -1)
            pick = jnp.where(row == local_e * BS + lax.rem(lane, BS), 1.0, 0.0).astype(BF16)
            c = jnp.dot(occ_ref[...], pick, preferred_element_type=F32)
            for hb in range(4):
                keep = jnp.where(place == hb, 1.0, 0.0)
                for m2 in range(2):
                    part = jnp.where(own // BS == m2, c, 0.0) * keep
                    at = (hb * 2 + m2) * BS
                    weights[at : at + BS, s * 128 : (s + 1) * 128] = part.astype(BF16)

    for j in range(32):
        wide[:, j] = x_ref[:, :, j * 128 : (j + 1) * 128].astype(F32)
    flat = wide.reshape(PB * 32 * SLOT, 128)
    for s in range(SLOT):
        rhs[:, s * 128 : (s + 1) * 128] = flat[pl.ds(s, PB * 32, stride=SLOT), :].astype(BF16)
    prod[...] = lax.dot_general(
        weights[...], rhs[...], (((1,), (1,)), ((), ())), preferred_element_type=F32
    )
    lane = lax.broadcasted_iota(jnp.int32, (NOCC, 128), 1)
    low64 = lane < 64
    low32 = lax.rem(lane, 64) < 32
    for h, ref in ((0, mine_ref), (1, other_ref)):
        out = ref.reshape(NOCC * PB, 128)
        for q in range(PB // 4):
            t = [prod[(h * 4 + k) * BS : (h * 4 + k + 1) * BS, q * 128 : (q + 1) * 128] for k in range(4)]
            r = [pltpu.roll(v, 64, 1) for v in t]
            a0 = jnp.where(low64, t[0], r[2])
            a2 = jnp.where(low64, r[0], t[2])
            a1 = jnp.where(low64, t[1], r[3])
            a3 = jnp.where(low64, r[1], t[3])
            for p, (u, v) in enumerate(((a0, a1), (a2, a3))):
                out[pl.ds(q * 4 + p * 2, NOCC, stride=PB), :] = jnp.where(low32, u, pltpu.roll(v, 32, 1))
                out[pl.ds(q * 4 + p * 2 + 1, NOCC, stride=PB), :] = jnp.where(low32, pltpu.roll(u, 96, 1), v)


def half_transform(integrals, pair_blocks, occ, start, size):
    first = start // PB
    out = jax.ShapeDtypeStruct((NOCC, size, 128), F32)
    block = pl.BlockSpec((NOCC, PB, 128), lambda g, pairs: (0, g, 0))
    return pl.pallas_call(
        half_kernel,
        out_shape=(out, out),
        grid_spec=pltpu.PrefetchScalarGridSpec(
            num_scalar_prefetch=1,
            grid=(size // PB,),
            in_specs=[
                pl.BlockSpec((PB, SLOT, BS * BS), lambda g, pairs: (g + first, 0, 0)),
                pl.BlockSpec((NOCC, 8 * BS), lambda g, pairs: (0, 0)),
            ],
            out_specs=(block, block),
            scratch_shapes=[
                pltpu.VMEM((8 * BS, SLOT * 128), BF16),
                pltpu.VMEM((PB, 32, SLOT, 128), F32),
                pltpu.VMEM((PB * 32, SLOT * 128), BF16),
                pltpu.VMEM((8 * BS, PB * 32), F32),
            ],
        ),
        compiler_params=pltpu.CompilerParams(vmem_limit_bytes=56 << 20),
        cost_estimate=pl.CostEstimate(flops=2 * size * 32 * 1024 * 512, bytes_accessed=size * 131072, transcendentals=0),
        name="half_transform",
    )(pair_blocks, integrals, occ)


def load(src, dst, sem, parts):
    step = src.shape[0] // parts
    return [
        pltpu.make_async_copy(src.at[pl.ds(k * step, step)], dst.at[pl.ds(k * step, step)], sem.at[k])
        for k in range(parts)
    ]


def tiles(metric_ref, rows, sem, start, size):
    return [
        pltpu.make_async_copy(
            metric_ref.at[:, pl.ds(start, size), pl.ds(n * TILE, TILE)], rows.at[:, :, pl.ds(n * TILE, TILE)], sem.at[n]
        )
        for n in range(NAUX // TILE)
    ]


def turn(buf, high, low):
    for r in range(4):
        t = jnp.concatenate([buf[a * 4 + r] for a in range(GROUPS)], axis=0).T
        top = t.astype(BF16)
        high[r * 128 : (r + 1) * 128, :] = top
        if low is not None:
            low[r * 128 : (r + 1) * 128, :] = (t - top.astype(F32)).astype(BF16)


def fit_kernel(start, size, own_ref, oth_ref, metric_ref, fit_ref, rows, buf, high, low, sem, hsem):
    depth = GROUPS * size
    metric = tiles(metric_ref, rows, sem, start, size)
    sides = [load(ref, buf.at[k], hsem.at[k], 4) for k, ref in enumerate((own_ref, oth_ref))]
    for c in (*sides[0], *sides[1], *metric):
        c.start()
    for k in range(2):
        for c in sides[k]:
            c.wait()
        turn(buf.at[k], high.at[k], low.at[k])
    for n in range(NAUX // TILE):
        metric[n].wait()
        m = rows[:, :, n * TILE : (n + 1) * TILE].reshape(depth, TILE)
        for k in range(2):
            fit_ref[k, :, n * TILE : (n + 1) * TILE] = jnp.dot(
                high[k], m, preferred_element_type=F32
            ) + jnp.dot(low[k], m, preferred_element_type=F32)


def first_fit(own, oth, metric, start, size):
    depth = GROUPS * size
    hbm = pl.BlockSpec(memory_space=pl.ANY)
    return pl.pallas_call(
        functools.partial(fit_kernel, start, size),
        out_shape=jax.ShapeDtypeStruct((2, 512, NAUX), F32),
        in_specs=[hbm, hbm, hbm],
        out_specs=pl.BlockSpec(memory_space=pltpu.VMEM),
        scratch_shapes=[
            pltpu.VMEM((GROUPS, size, NAUX), BF16),
            pltpu.VMEM((2, 64, size, 128), F32),
            pltpu.VMEM((2, 512, depth), BF16),
            pltpu.VMEM((2, 512, depth), BF16),
            pltpu.SemaphoreType.DMA((NAUX // TILE,)),
            pltpu.SemaphoreType.DMA((2, 4)),
        ],
        compiler_params=pltpu.CompilerParams(vmem_limit_bytes=46 << 20),
        cost_estimate=pl.CostEstimate(flops=4 * depth * NAUX * 1024, bytes_accessed=24 << 20, transcendentals=0),
        name="first_fit",
    )(own, oth, metric)


def own_kernel(start, size, h_ref, part_ref, metric_ref, fit_ref, rows, buf, part, high, sem, hsem, psem):
    depth = GROUPS * size
    metric = tiles(metric_ref, rows, sem, start, size)
    side = load(h_ref, buf, hsem, 4)
    add = pltpu.make_async_copy(part_ref.at[0], part, psem)
    for c in (*side, *metric, add):
        c.start()
    for c in side:
        c.wait()
    turn(buf, high, None)
    add.wait()
    for n in range(NAUX // TILE):
        metric[n].wait()
        at = slice(n * TILE, (n + 1) * TILE)
        m = rows[:, :, at].reshape(depth, TILE)
        f = part[:, at] + jnp.dot(high[...], m, preferred_element_type=F32)
        top = f.astype(BF16)
        fit_ref[0, :, at] = top
        fit_ref[1, :, at] = (f - top.astype(F32)).astype(BF16)


def own_fit(own, part, metric, start, size):
    depth = GROUPS * size
    hbm = pl.BlockSpec(memory_space=pl.ANY)
    return pl.pallas_call(
        functools.partial(own_kernel, start, size),
        out_shape=jax.ShapeDtypeStruct((2, 512, NAUX), BF16),
        in_specs=[hbm, hbm, hbm],
        out_specs=pl.BlockSpec(memory_space=pltpu.VMEM),
        scratch_shapes=[
            pltpu.VMEM((GROUPS, size, NAUX), BF16),
            pltpu.VMEM((64, size, 128), F32),
            pltpu.VMEM((512, NAUX), F32),
            pltpu.VMEM((512, depth), BF16),
            pltpu.SemaphoreType.DMA((NAUX // TILE,)),
            pltpu.SemaphoreType.DMA((4,)),
            pltpu.SemaphoreType.DMA,
        ],
        compiler_params=pltpu.CompilerParams(vmem_limit_bytes=46 << 20),
        cost_estimate=pl.CostEstimate(flops=2 * depth * NAUX * 512, bytes_accessed=16 << 20, transcendentals=0),
        name="own_fit",
    )(own, part, metric)


def last_kernel(
    start, size, h_ref, part_ref, fit_ref, metric_ref, out_ref, rows, buf, part, own, high, fit, sem, hsem, psem
):
    depth = GROUPS * size
    metric = tiles(metric_ref, rows, sem, start, size)
    side = load(h_ref, buf, hsem, 4)
    add = pltpu.make_async_copy(part_ref.at[1], part, psem.at[0])
    mine = pltpu.make_async_copy(fit_ref, own, psem.at[1])
    for c in (*side, *metric, add, mine):
        c.start()
    for c in side:
        c.wait()
    turn(buf, high, None)
    add.wait()
    for n in range(NAUX // TILE):
        metric[n].wait()
        at = slice(n * TILE, (n + 1) * TILE)
        m = rows[:, :, at].reshape(depth, TILE)
        fit[:, at] = (part[:, at] + jnp.dot(high[...], m, preferred_element_type=F32)).astype(BF16)
    mine.wait()

    core = lax.axis_index("col")
    for other in range(2):
        half = lax.rem(core + other, 2)
        f = fit[...] if other else own[0]
        k = lax.dot_general(f, own[0], (((1,), (1,)), ((), ())), preferred_element_type=F32)
        k = k + lax.dot_general(f, own[1], (((1,), (1,)), ((), ())), preferred_element_type=F32)
        part[:, :512] = k
        for y in range(4):
            for b in range(2):
                for z in range(4):
                    chip = (y * 4 + half * 2 + b) * 4 + z
                    for c in range(2):
                        for m2 in range(2):
                            top = y * 128 + b * 64 + m2 * 32 + c * 16
                            out_ref[chip * 2 + c, m2 * 16 : (m2 + 1) * 16, :] = part[
                                top : top + 16, z * 128 : (z + 1) * 128
                            ]


def last_fit(oth, part, fit, metric, start, size):
    depth = GROUPS * size
    hbm = pl.BlockSpec(memory_space=pl.ANY)
    return pl.pallas_call(
        functools.partial(last_kernel, start, size),
        out_shape=jax.ShapeDtypeStruct((128, 32, 128), F32),
        in_specs=[hbm, hbm, hbm, hbm],
        out_specs=pl.BlockSpec(memory_space=pltpu.VMEM),
        scratch_shapes=[
            pltpu.VMEM((GROUPS, size, NAUX), BF16),
            pltpu.VMEM((64, size, 128), F32),
            pltpu.VMEM((512, NAUX), F32),
            pltpu.VMEM((2, 512, NAUX), BF16),
            pltpu.VMEM((512, depth), BF16),
            pltpu.VMEM((512, NAUX), BF16),
            pltpu.SemaphoreType.DMA((NAUX // TILE,)),
            pltpu.SemaphoreType.DMA((4,)),
            pltpu.SemaphoreType.DMA((2,)),
        ],
        compiler_params=pltpu.CompilerParams(vmem_limit_bytes=46 << 20),
        cost_estimate=pl.CostEstimate(flops=2 * depth * NAUX * 512, bytes_accessed=16 << 20, transcendentals=0),
        name="last_fit",
    )(oth, part, fit, metric)


def sum_kernel(x_ref, out_ref):
    lane_in = lax.broadcasted_iota(jnp.int32, (128, 128), 0)
    lane_out = lax.broadcasted_iota(jnp.int32, (128, 128), 1)
    src = (lane_out // 64) * 64 + lax.rem(lane_out, 2) * 32 + lax.rem(lane_out, 64) // 2
    right = jnp.where(lane_in == src, 1.0, 0.0)
    row_out = lax.broadcasted_iota(jnp.int32, (32, 32), 0)
    row_in = lax.broadcasted_iota(jnp.int32, (32, 32), 1)
    left = jnp.where(row_in == lax.rem(row_out, 2) * 16 + row_out // 2, 1.0, 0.0)
    for h in range(2):
        total = jnp.sum(x_ref[:, h], axis=0)
        total = jnp.dot(total, right, precision=lax.Precision.HIGHEST, preferred_element_type=F32)
        total = jnp.dot(left, total, precision=lax.Precision.HIGHEST, preferred_element_type=F32)
        out_ref[:, h * 128 : (h + 1) * 128] = total


def sum_chips(x):
    return pl.pallas_call(
        sum_kernel,
        out_shape=jax.ShapeDtypeStruct((32, 256), F32),
        compiler_params=pltpu.CompilerParams(vmem_limit_bytes=16 << 20),
        name="sum_chips",
    )(x.reshape(64, 2, 32, 128))


def body(integrals, pair_blocks, occupied, metric):
    occ = occupied.T
    metric = metric.reshape(GROUPS, AUX, NAUX)
    swap = [(0, 1), (1, 0)]
    received = []
    for start, size in CHUNKS:
        mine, other = half_transform(integrals, pair_blocks, occ, start, size)
        h = mine + lax.ppermute(other, "col", swap)
        h, pair_blocks = lax.optimization_barrier((h, pair_blocks))
        received.append(lax.all_to_all(h, ("aux", "row"), 0, 0))
    own, last = received
    part = first_fit(own, lax.ppermute(own, "col", swap), metric, *CHUNKS[0])
    last, part = lax.optimization_barrier((last, part))
    crossed = lax.ppermute(last, "col", swap)
    fit = own_fit(last, part, metric, *CHUNKS[1])
    k = last_fit(crossed, part, fit, metric, *CHUNKS[1])
    k = lax.all_to_all(k, ("aux", "row", "col"), 0, 0)
    return sum_chips(k).T


def solution(mesh):
    return jax.shard_map(
        body,
        mesh=mesh,
        in_specs=(P("aux", ("row", "col"), None), P(None, ("row", "col")), P("col", None), P()),
        out_specs=P("row", ("aux", "col")),
        check_vma=False,
    )
```

time: 579 us -> 179 us (0.31)
  waiting for transfers between devices: 289 us -> 38.5 us
  matrix products: 106 us -> 0 us
  Pallas kernels: 0 us -> 70.5 us
  local copies, waits for them, and re-layouts: 70.8 us -> 2.37 us
  blocking collectives: 68 us -> 35.6 us
  loops' own time: 28.7 us -> 0 us
  starting transfers between devices: 0.09 us -> 24 us
  between operations: 13.1 us -> 0.06 us
  other arithmetic: 0 us -> 7.1 us
    all_gather x1 -> x0, waiting for transfers between devices: 187 us -> none  [body(): lax.all_gather(fitted, 'row', axis=2, tiled=True)]
    dot_general x10 -> x0, matrix products: 106 us -> none  [the longest x1 45.5 us: body(): jnp.einsum('qp,ipm->iqm', metric_wide, lax.all_to_all(summed, 'aux', spli...]
    reduce_scatter x2 -> x0, waiting for transfers between devices: 102 us -> none  [the longest x1 76.8 us: body(): lax.psum_scatter(contrib, ('aux', 'col'), scatter_dimension=1, tiled=True)]
    pallas_call x0 -> x6, Pallas kernels: none -> 70.5 us  [the longest x2 22.4 us: half_transform(): pl.pallas_call(half_kernel, out_shape=(out, out), grid_spec=pltpu.Prefetc...]
    while x2 -> x0, local copies, waits for them, and re-layouts: 39.3 us -> none  [body(): lax.scan(add_slot, start, jnp.arange(slot_count, dtype=jnp.int32))]
    all_to_all x0 -> x2, waiting for transfers between devices: none -> 33.8 us  [body(): received.append(lax.all_to_all(h, ('aux', 'row'), 0, 0))]
    all_to_all x1, blocking collectives: 68 us -> 35.6 us  [body(): k = lax.all_to_all(k, ('aux', 'row', 'col'), 0, 0)]
    another operation x1 -> x0, loops' own time: 28.7 us -> none  [body(): lax.scan(add_slot, start, jnp.arange(slot_count, dtype=jnp.int32))]
  transfers between devices with their start and end apart: 3 -> 6, of which waited for: 3 -> 3; matrix products, arithmetic and copies ran while one was open for 0% -> 2% of each run, Pallas kernels for 0% -> 24%
where the time goes in v1:
time: 179 us; the launch traced here: 178 us
  Pallas kernels  70.5 us (39%)
  waiting for transfers between devices  38.5 us (22%)
  blocking collectives  35.6 us (20%)
  starting transfers between devices  24 us (13%)
  other arithmetic  7.1 us (4%)
  local copies, waits for them, and re-layouts  2.37 us (1%)
    all_to_all x1, blocking collectives, body(): k = lax.all_to_all(k, ('aux', 'row', 'col'), 0, 0)  35.6 us
    all_to_all x2, waiting for transfers between devices, body(): received.append(lax.all_to_all(h, ('aux', 'row'), 0, 0))  33.8 us
    pallas_call x2, Pallas kernels, half_transform(): pl.pallas_call(half_kernel, out_shape=(out, out), grid_spec=pltpu.Prefetc...  22.4 us
    pallas_call x1, Pallas kernels, first_fit(): pl.pallas_call(functools.partial(fit_kernel, start, size), out_shape=jax....  21.6 us
    all_to_all x2, starting transfers between devices, body(): received.append(lax.all_to_all(h, ('aux', 'row'), 0, 0))  17.8 us
    pallas_call x1, Pallas kernels, last_fit(): pl.pallas_call(functools.partial(last_kernel, start, size), out_shape=jax...  15.3 us
    pallas_call x1, Pallas kernels, own_fit(): pl.pallas_call(functools.partial(own_kernel, start, size), out_shape=jax....  9.8 us
    add x2, other arithmetic, body(): h = mine + lax.ppermute(other, 'col', swap)  7.1 us
  transfers between devices with their start and end apart: 6, of which 3 were waited for; matrix products, arithmetic and copies ran while one was open for 2% of the time, Pallas kernels for 24%

profile of v1, /device:TPU:1, one launch (start us, length us, event | category | flops | bytes accessed | tf_op | source)
XLA Modules:
  0.0 178.2 jit_solution(11905374597249890297)
XLA Ops:
  0.0 11.2 %half_transform.2 = (f32[64,80,128]{2,1,0:T(8,128)}, f32[64,80,128]{2,1,0:T(8,128)}) custom-call(s32[2,8]{1,0:T(2,128)} %pairs.2, bf16[160,8,4096]{2,1,0:T(8,128)(2,1)} %x_ref.3, bf16[64,512]{1,0:T(8,128)(2,1)} %bitcast.8), custom_call_target="tpu_custom_call" | custom-call | flops 2684354560 | bytes 10485760 | tf_op jit(solution)/shard_map/half_transform/pallas_call | solution.py:74
  11.2 1.4 collective-permute-start
  12.6 4.7 %collective-permute-done = f32[64,80,128]{2,1,0:T(8,128)S(1)} collective-permute-done((f32[64,80,128]{2,1,0:T(8,128)}, f32[64,80,128]{2,1,0:T(8,128)S(1)}, u32[]{:S(2)}, u32[]{:S(2)}) %collective-permute-start) | collective-permute-done | bytes 2621472 | tf_op jit(solution)/shard_map/ppermute | solution.py:305
  17.4 3.6 %add.6 = f32[64,80,128]{2,1,0:T(8,128)} add(f32[64,80,128]{2,1,0:T(8,128)} %get-tuple-element.14, f32[64,80,128]{2,1,0:T(8,128)S(1)} %collective-permute-done) | non-fusion elementwise | flops 655360 | bytes 7864320 | tf_op jit(solution)/shard_map/add | solution.py:305
  20.9 11.5 %all-to-all-start.1 = ((f32[64,80,128]{2,1,0:T(8,128)}), f32[64,80,128]{2,1,0:T(8,128)}, u32[]{:S(2)}, u32[]{:S(2)}) async-start(f32[64,80,128]{2,1,0:T(8,128)} %add.6), calls=%async_computation.1 | async-start | bytes 5242880 | tf_op jit(solution)/shard_map/all_to_all | solution.py:307
  32.4 11.2 %half_transform.3 = (f32[64,80,128]{2,1,0:T(8,128)}, f32[64,80,128]{2,1,0:T(8,128)}) custom-call(s32[2,8]{1,0:T(2,128)} %pairs.2, bf16[160,8,4096]{2,1,0:T(8,128)(2,1)} %x_ref.3, bf16[64,512]{1,0:T(8,128)(2,1)} %bitcast.9), custom_call_target="tpu_custom_call" | custom-call | flops 2684354560 | bytes 10485760 | tf_op jit(solution)/shard_map/half_transform/pallas_call | solution.py:74
  43.6 0.6 collective-permute-start.1
  44.3 21.6 %all-to-all-done.1.own_ref = f32[64,80,128]{2,1,0:T(8,128)} async-done(((f32[64,80,128]{2,1,0:T(8,128)}), f32[64,80,128]{2,1,0:T(8,128)}, u32[]{:S(2)}, u32[]{:S(2)}) %all-to-all-start.1) | async-done | bytes 2621472 | tf_op jit(solution)/shard_map/all_to_all | solution.py:307
  65.9 2.4 %collective-permute-start.2 = (f32[64,80,128]{2,1,0:T(8,128)}, f32[64,80,128]{2,1,0:T(8,128)}, u32[]{:S(2)}, u32[]{:S(2)}) collective-permute-start(f32[64,80,128]{2,1,0:T(8,128)} %all-to-all-done.1.own_ref), channel_id=1, source_target_pairs={{0,1},{1,0},{2,3},{3,2},{4,5},{5,4},{6,7},{7,6},{8,9},{9,8},{10,11... | collective-permute-start | bytes 7864328 | tf_op jit(solution)/shard_map/ppermute | solution.py:309
  68.3 0.0 collective-permute-done.1
  68.3 3.5 %add.7 = f32[64,80,128]{2,1,0:T(8,128)} add(f32[64,80,128]{2,1,0:T(8,128)} %get-tuple-element.17, f32[64,80,128]{2,1,0:T(8,128)S(1)} %collective-permute-done.1) | non-fusion elementwise | flops 655360 | bytes 7864320 | tf_op jit(solution)/shard_map/add | solution.py:305
  71.8 6.3 %all-to-all-start = ((f32[64,80,128]{2,1,0:T(8,128)}), f32[64,80,128]{2,1,0:T(8,128)S(1)}, u32[]{:S(2)}, u32[]{:S(2)}) async-start(f32[64,80,128]{2,1,0:T(8,128)} %add.7), calls=%async_computation | async-start | bytes 5242880 | tf_op jit(solution)/shard_map/all_to_all | solution.py:307
  78.1 0.0 collective-permute-done.2.oth_ref
  78.1 21.6 %first_fit.1.part_ref = f32[2,512,2560]{2,1,0:T(8,128)} custom-call(f32[64,80,128]{2,1,0:T(8,128)} %all-to-all-done.1.own_ref, f32[64,80,128]{2,1,0:T(8,128)} %collective-permute-done.2.oth_ref, bf16[16,160,2560]{2,1,0:T(8,128)(2,1)} %bitcast.5), custom_call_target="tpu_custom_call" | custom-call | flops 13421772800 | bytes 25165824 | tf_op jit(solution)/shard_map/first_fit/pallas_call | solution.py:146
  99.8 12.2 %all-to-all-done.h_ref = f32[64,80,128]{2,1,0:T(8,128)S(1)} async-done(((f32[64,80,128]{2,1,0:T(8,128)}), f32[64,80,128]{2,1,0:T(8,128)S(1)}, u32[]{:S(2)}, u32[]{:S(2)}) %all-to-all-start) | async-done | bytes 2621472 | tf_op jit(solution)/shard_map/all_to_all | solution.py:307
  112.0 1.8 %collective-permute-start.3 = (f32[64,80,128]{2,1,0:T(8,128)S(1)}, f32[64,80,128]{2,1,0:T(8,128)S(1)}, u32[]{:S(2)}, u32[]{:S(2)}) collective-permute-start(f32[64,80,128]{2,1,0:T(8,128)S(1)} %all-to-all-done.h_ref), channel_id=1, source_target_pairs={{0,1},{1,0},{2,3},{3,2},{4,5},{5,4},{6,7},{7,6},{8,9},{9,8},{10,11... | collective-permute-start | bytes 7864328 | tf_op jit(solution)/shard_map/ppermute | solution.py:311
  113.8 9.8 %own_fit.1.fit_ref = bf16[2,512,2560]{2,1,0:T(8,128)(2,1)S(1)} custom-call(f32[64,80,128]{2,1,0:T(8,128)S(1)} %all-to-all-done.h_ref, f32[2,512,2560]{2,1,0:T(8,128)} %first_fit.1.part_ref, bf16[16,160,2560]{2,1,0:T(8,128)(2,1)} %bitcast.6), custom_call_target="tpu_custom_call" | custom-call | flops 3355443200 | bytes 16777216 | tf_op jit(solution)/shard_map/own_fit/pallas_call | solution.py:189
  123.6 0.0 copy-start
  123.6 2.4 %copy-done = bf16[2,512,2560]{2,1,0:T(8,128)(2,1)} copy-done((bf16[2,512,2560]{2,1,0:T(8,128)(2,1)}, bf16[2,512,2560]{2,1,0:T(8,128)(2,1)S(1)}, u32[]{:S(2)}) %copy-start) | copy-done | bytes 5242904
  126.0 0.0 collective-permute-done.3.h_ref
  126.0 15.3 %last_fit.1 = f32[128,32,128]{2,1,0:T(8,128)S(1)} custom-call(f32[64,80,128]{2,1,0:T(8,128)S(1)} %collective-permute-done.3.h_ref, f32[2,512,2560]{2,1,0:T(8,128)} %first_fit.1.part_ref, bf16[2,512,2560]{2,1,0:T(8,128)(2,1)} %copy-done, bf16[16,160,2560]{2,1,0:T(8,128)(2,1)} %bitcast.7), custom_call_target="tpu_custom_call" | custom-call | flops 3355443200 | bytes 16777216 | tf_op jit(solution)/shard_map/last_fit/pallas_call | solution.py:252
  141.3 35.6 %all_to_all.15 = f32[128,32,128]{2,1,0:T(8,128)S(1)} all-to-all(f32[128,32,128]{2,1,0:T(8,128)S(1)} %last_fit.1), channel_id=1, replica_groups=mesh['aux'=16,'row'=4,'col'=2] {'aux','row','col'}, dimensions={0} | all-to-all | bytes 4194304 | tf_op jit(solution)/shard_map/all_to_all | solution.py:314
  176.9 1.3 sum_chips.1
Async XLA Ops:
  11.2 6.2 %collective-permute-start = (f32[64,80,128]{2,1,0:T(8,128)}, f32[64,80,128]{2,1,0:T(8,128)S(1)}, u32[]{:S(2)}, u32[]{:S(2)}) collective-permute-start(f32[64,80,128]{2,1,0:T(8,128)} %get-tuple-element.15), channel_id=1, source_target_pairs={{0,1},{1,0},{2,3},{3,2},{4,5},{5,4},{6,7},{7,6},{8,9},{9,8},{10,11... | collective-permute-start | bytes 7864328 | tf_op jit(solution)/shard_map/ppermute | solution.py:305
  20.9 44.9 %all-to-all-start.1 = ((f32[64,80,128]{2,1,0:T(8,128)}), f32[64,80,128]{2,1,0:T(8,128)}, u32[]{:S(2)}, u32[]{:S(2)}) async-start(f32[64,80,128]{2,1,0:T(8,128)} %add.6), calls=%async_computation.1 | async-start | bytes 5242880 | tf_op jit(solution)/shard_map/all_to_all | solution.py:307
  43.6 24.6 %collective-permute-start.1 = (f32[64,80,128]{2,1,0:T(8,128)}, f32[64,80,128]{2,1,0:T(8,128)S(1)}, u32[]{:S(2)}, u32[]{:S(2)}) collective-permute-start(f32[64,80,128]{2,1,0:T(8,128)} %get-tuple-element.18), channel_id=1, source_target_pairs={{0,1},{1,0},{2,3},{3,2},{4,5},{5,4},{6,7},{7,6},{8,9},{9,8},{10,11... | collective-permute-start | bytes 7864328 | tf_op jit(solution)/shard_map/ppermute | solution.py:305
  65.9 12.2 %collective-permute-start.2 = (f32[64,80,128]{2,1,0:T(8,128)}, f32[64,80,128]{2,1,0:T(8,128)}, u32[]{:S(2)}, u32[]{:S(2)}) collective-permute-start(f32[64,80,128]{2,1,0:T(8,128)} %all-to-all-done.1.own_ref), channel_id=1, source_target_pairs={{0,1},{1,0},{2,3},{3,2},{4,5},{5,4},{6,7},{7,6},{8,9},{9,8},{10,11... | collective-permute-start | bytes 7864328 | tf_op jit(solution)/shard_map/ppermute | solution.py:309
  71.8 40.2 %all-to-all-start = ((f32[64,80,128]{2,1,0:T(8,128)}), f32[64,80,128]{2,1,0:T(8,128)S(1)}, u32[]{:S(2)}, u32[]{:S(2)}) async-start(f32[64,80,128]{2,1,0:T(8,128)} %add.7), calls=%async_computation | async-start | bytes 5242880 | tf_op jit(solution)/shard_map/all_to_all | solution.py:307
  112.0 14.0 %collective-permute-start.3 = (f32[64,80,128]{2,1,0:T(8,128)S(1)}, f32[64,80,128]{2,1,0:T(8,128)S(1)}, u32[]{:S(2)}, u32[]{:S(2)}) collective-permute-start(f32[64,80,128]{2,1,0:T(8,128)S(1)} %all-to-all-done.h_ref), channel_id=1, source_target_pairs={{0,1},{1,0},{2,3},{3,2},{4,5},{5,4},{6,7},{7,6},{8,9},{9,8},{10,11... | collective-permute-start | bytes 7864328 | tf_op jit(solution)/shard_map/ppermute | solution.py:311
  123.6 2.4 %copy-start = (bf16[2,512,2560]{2,1,0:T(8,128)(2,1)}, bf16[2,512,2560]{2,1,0:T(8,128)(2,1)S(1)}, u32[]{:S(2)}) copy-start(bf16[2,512,2560]{2,1,0:T(8,128)(2,1)S(1)} %own_fit.1.fit_ref) | copy-start | bytes 15728644
